TPU v7x, 32 devices: a whole 2x2x4 slice. The times are simulated.
32 devices in a mesh: grp: 4 (over x, core), dp: 8 (over z, y).
Axes of the slice: x: 2, y: 2, z: 4, core: 2. Of those that a mesh axis runs over, the one named last changes fastest.
Arguments:
- photo_vectors_raw: bfloat16 [32768, 768], P(('grp', 'dp')), may hold values from -0.21875 to 0.21875
- sentence_vectors_raw: bfloat16 [32768, 768], P(('grp', 'dp')), may hold values from -0.21875 to 0.21875
- companion_index: int32 [32, 1024], P(('grp', 'dp')), may hold values from 0 to 1023, each once within a row
- exponent_of_sharpness: float32 [1], replicated, may hold values from 1 to 2.3
- affinity_offset: float32 [1], replicated, may hold values from -4 to -1
Outputs:
- image_grad: float32 [32768, 768], P(('grp', 'dp'))
- text_grad: float32 [32768, 768], P(('grp', 'dp'))
Inputs may be any that keep to these rules, and one draw needn't show every extreme that they name: Each row of companion_index is a permutation of 0 to 1023.
All inputs are finite; a program needn't handle non-finite values.
Results may differ from a plain program's by a relative error of at most 0.0055.
Values may be sent and summed in bfloat16 or wider, within the bound.
A program may use at most 128 MiB of HBM per device.

v0:
```python
import jax
import jax.numpy as jnp
from jax import lax
from jax.sharding import PartitionSpec as P


def passed_along(x, axis, by):
    devices = lax.axis_size(axis)
    return lax.ppermute(x, axis, [(i, (i + by) % devices) for i in range(devices)])


def unit_rows(raw):
    values = raw.astype(jnp.float32)
    inverse_norm = lax.rsqrt(jnp.sum(values * values, -1, keepdims=True) + 1e-06)
    return (values * inverse_norm, inverse_norm)


def gradient_panel(picture_rows, caption_rows, matching_pairs, sharpness_factor, block_distance):
    score_matrix = (
        sharpness_factor * jnp.dot(picture_rows, caption_rows.T, preferred_element_type=jnp.float32)
        + block_distance
    )
    if matching_pairs is None:
        target_labels = -1.0
    else:
        target_labels = jnp.where(matching_pairs, 1.0, -1.0)
    return (
        sharpness_factor * -target_labels * jax.nn.sigmoid(-target_labels * score_matrix)
    ).astype(jnp.bfloat16)


def unit_backward(grad, unit, inverse_norm):
    return inverse_norm * (grad - unit * jnp.sum(unit * grad, -1, keepdims=True))


def similarity_entries(left, right):
    return jnp.dot(left, right, preferred_element_type=jnp.float32)


def local(
    photo_vectors_raw, sentence_vectors_raw, companion_index, exponent_of_sharpness, affinity_offset
):
    sharpness_factor = jnp.exp(exponent_of_sharpness[0])
    block_distance = affinity_offset[0]
    image_unit, image_norm = unit_rows(photo_vectors_raw)
    text_unit, text_norm = unit_rows(sentence_vectors_raw)
    picture_rows = image_unit.astype(jnp.bfloat16)
    caption_rows = text_unit.astype(jnp.bfloat16)
    row_count = picture_rows.shape[0]
    matching_pairs = companion_index[0][:, None] == jnp.arange(row_count, dtype=jnp.int32)[None, :]
    local_panel = gradient_panel(
        picture_rows, caption_rows, matching_pairs, sharpness_factor, block_distance
    )
    preceding_block = passed_along(caption_rows, ("grp", "dp"), 1)
    following_block = passed_along(caption_rows, ("grp", "dp"), -1)
    leftward_panel = gradient_panel(
        picture_rows, preceding_block, None, sharpness_factor, block_distance
    )
    rightward_panel = gradient_panel(
        picture_rows, following_block, None, sharpness_factor, block_distance
    )
    image_part = (
        similarity_entries(local_panel, caption_rows)
        + similarity_entries(leftward_panel, preceding_block)
        + similarity_entries(rightward_panel, following_block)
    )
    text_left = similarity_entries(leftward_panel.T, picture_rows)
    text_right = similarity_entries(rightward_panel.T, picture_rows)
    from_after = passed_along(text_left.astype(jnp.bfloat16), ("grp", "dp"), -1).astype(
        text_left.dtype
    )
    from_before = passed_along(text_right.astype(jnp.bfloat16), ("grp", "dp"), 1).astype(
        text_right.dtype
    )
    text_part = similarity_entries(local_panel.T, picture_rows) + from_after + from_before
    image_grad = unit_backward(image_part, image_unit, image_norm)
    text_grad = unit_backward(text_part, text_unit, text_norm)
    return (image_grad, text_grad)


def solution(mesh):
    placed = (P(("grp", "dp"), None), P(("grp", "dp"), None), P(("grp", "dp"), None), P(), P())
    return jax.shard_map(
        local,
        mesh=mesh,
        in_specs=placed,
        out_specs=(P(("grp", "dp"), None), P(("grp", "dp"), None)),
        check_vma=False,
    )
```

profile of v0, /device:TPU:0, one launch (start us, length us, event | category | flops | bytes accessed | tf_op | source)
XLA Modules:
  0.0 168.3 jit_solution(15590574016053185608)
XLA Ops:
  0.6 1.7 %copy.8 = bf16[1024,768]{0,1:T(8,128)(2,1)S(1)} copy(bf16[1024,768]{1,0:T(8,128)(2,1)} %param.6) | data formatting | bytes 3145728 | tf_op args[1]
  2.4 0.4 fusion.13
  2.7 1.6 fusion.2
  4.3 0.0 copy-start
  4.3 6.4 %collective-permute-start.1 = (bf16[1024,768]{0,1:T(8,128)(2,1)}, bf16[1024,768]{0,1:T(8,128)(2,1)}, u32[]{:S(2)}, u32[]{:S(2)}) collective-permute-start(bf16[1024,768]{0,1:T(8,128)(2,1)} %fusion.2), channel_id=1, source_target_pairs={{0,31},{1,0},{2,1},{3,2},{4,3},{5,4},{6,5},{7,6},{8,7},{9,8},{10,9... | collective-permute-start | bytes 4718600 | tf_op jit(solution)/shard_map/ppermute | solution.py:9
  10.6 0.0 collective-permute-start
  10.7 1.7 %copy.7 = bf16[1024,768]{0,1:T(8,128)(2,1)S(1)} copy(bf16[1024,768]{1,0:T(8,128)(2,1)} %param.5) | data formatting | bytes 3145728 | tf_op args[0]
  12.4 0.4 fusion.9
  14.1 0.0 copy-done
  14.1 4.9 %multiply_convert_fusion.2 = bf16[1024,1024]{1,0:T(8,128)(2,1)S(1)} fusion(bf16[1024,768]{0,1:T(8,128)(2,1)} %fusion.2, f32[]{:T(128)} %bitcast.15, s32[1024]{0:T(1024)S(1)} %bitcast.18, f32[]{:T(128)} %bitcast, bf16[1024,768]{0,1:T(8,128)(2,1)S(1)} %copy.7, f32[1024]{0:T(1024)S(1)} %add_rsqrt_fusion.1), kind=kOutput, calls=%fused_computation.2 | convolution fusion | flops 1625554944 | bytes 5251080 | tf_op jit(solution)/shard_map/dot_general | solution.py:20
  19.0 0.0 copy-start.1
  19.0 4.0 %fusion.21 = f32[1024,768]{0,1:T(8,128)S(1)} fusion(bf16[1024,1024]{1,0:T(8,128)(2,1)S(1)} %multiply_convert_fusion.2, bf16[1024,768]{0,1:T(8,128)(2,1)} %fusion.2), kind=kOutput, calls=%fused_computation.29 | convolution fusion | flops 1610612736 | bytes 6815744 | tf_op jit(solution)/shard_map/dot_general | solution.py:37
  23.0 0.0 copy-done.1
  23.0 52.6 %collective-permute-done.1 = bf16[1024,768]{0,1:T(8,128)(2,1)} collective-permute-done((bf16[1024,768]{0,1:T(8,128)(2,1)}, bf16[1024,768]{0,1:T(8,128)(2,1)}, u32[]{:S(2)}, u32[]{:S(2)}) %collective-permute-start.1) | collective-permute-done | bytes 1572896 | tf_op jit(solution)/shard_map/ppermute | solution.py:9
  75.7 4.0 %multiply_convert_fusion = bf16[1024,1024]{1,0:T(8,128)(2,1)S(1)} fusion(bf16[1024,768]{0,1:T(8,128)(2,1)} %collective-permute-done.1, f32[]{:T(128)} %bitcast.16, f32[]{:T(128)} %bitcast, bf16[1024,768]{0,1:T(8,128)(2,1)S(1)} %copy.7, f32[1024]{0:T(1024)S(1)} %add_rsqrt_fusion.1), kind=kOutput, calls=%fused_computation | convolution fusion | flops 1620312064 | bytes 5246984 | tf_op jit(solution)/shard_map/dot_general | solution.py:20
  79.6 3.0 %convolution_convert_fusion = bf16[1024,768]{0,1:T(8,128)(2,1)} fusion(bf16[1024,1024]{1,0:T(8,128)(2,1)S(1)} %multiply_convert_fusion, bf16[1024,768]{0,1:T(8,128)(2,1)S(1)} %copy.7, f32[1024]{0:T(1024)S(1)} %add_rsqrt_fusion.1), kind=kOutput, calls=%fused_computation.24 | convolution fusion | flops 1613758464 | bytes 5246976 | tf_op jit(solution)/shard_map/dot_general | solution.py:37
  82.7 0.0 collective-permute-start.3
  82.7 0.0 collective-permute-done
  82.7 4.0 %multiply_convert_fusion.1 = bf16[1024,1024]{1,0:T(8,128)(2,1)S(1)} fusion(bf16[1024,768]{0,1:T(8,128)(2,1)} %collective-permute-done, f32[]{:T(128)} %bitcast.17, f32[]{:T(128)} %bitcast, bf16[1024,768]{0,1:T(8,128)(2,1)S(1)} %copy.7, f32[1024]{0:T(1024)S(1)} %add_rsqrt_fusion.1), kind=kOutput, calls=%fused_computation.1 | convolution fusion | flops 1620312064 | bytes 5246984 | tf_op jit(solution)/shard_map/dot_general | solution.py:20
  86.7 3.0 %convolution_convert_fusion.1 = bf16[1024,768]{0,1:T(8,128)(2,1)} fusion(bf16[1024,1024]{1,0:T(8,128)(2,1)S(1)} %multiply_convert_fusion.1, bf16[1024,768]{0,1:T(8,128)(2,1)S(1)} %copy.7, f32[1024]{0:T(1024)S(1)} %add_rsqrt_fusion.1), kind=kOutput, calls=%fused_computation.25 | convolution fusion | flops 1613758464 | bytes 5246976 | tf_op jit(solution)/shard_map/dot_general | solution.py:37
  89.6 5.3 %collective-permute-start.2 = (bf16[1024,768]{0,1:T(8,128)(2,1)}, bf16[1024,768]{0,1:T(8,128)(2,1)}, u32[]{:S(2)}, u32[]{:S(2)}) collective-permute-start(bf16[1024,768]{0,1:T(8,128)(2,1)} %convolution_convert_fusion.1), channel_id=1, source_target_pairs={{0,31},{1,0},{2,1},{3,2},{4,3},{5,4},{6,5},{7,6},{8,7},{9,8},{10,9... | collective-permute-start | bytes 4718600 | tf_op jit(solution)/shard_map/ppermute | solution.py:9
  95.0 3.2 %fusion.22 = f32[1024,768]{0,1:T(8,128)S(1)} fusion(bf16[1024,1024]{1,0:T(8,128)(2,1)S(1)} %multiply_convert_fusion.1, bf16[1024,768]{0,1:T(8,128)(2,1)} %collective-permute-done), kind=kOutput, calls=%fused_computation.30 | convolution fusion | flops 1610612736 | bytes 6815744 | tf_op jit(solution)/shard_map/dot_general | solution.py:37
  98.2 3.6 %fusion.6 = (f32[1024]{0:T(1024)S(1)}, f32[1024,768]{0,1:T(8,128)S(1)}) fusion(bf16[1024,768]{0,1:T(8,128)(2,1)S(1)} %copy.7, f32[1024]{0:T(1024)S(1)} %add_rsqrt_fusion.1, bf16[1024,1024]{1,0:T(8,128)(2,1)S(1)} %multiply_convert_fusion, bf16[1024,768]{0,1:T(8,128)(2,1)} %collective-permute-done.1, f32[1024,768]{0,1:T(8,128)S(1)} %fusion.21, ...), kind=kOutput, calls=%fused_computation.14 | convolution fusion | flops 1615330304 | bytes 14688256 | tf_op jit(solution)/shard_map/dot_general | solution.py:37
  101.8 2.3 %fusion.8 = f32[1024,768]{0,1:T(8,128)} fusion(f32[1024,768]{0,1:T(8,128)S(1)} %get-tuple-element.5, bf16[1024,768]{0,1:T(8,128)(2,1)S(1)} %copy.7, f32[1024]{0:T(1024)S(1)} %get-tuple-element.4, f32[1024]{0:T(1024)S(1)} %add_rsqrt_fusion.1), kind=kLoop, calls=%fused_computation.16 | loop fusion | flops 3932160 | bytes 7872512 | tf_op jit(solution)/shard_map/mul | solution.py:33
  104.1 3.5 %copy.11 = f32[1024,768]{1,0:T(8,128)} copy(f32[1024,768]{0,1:T(8,128)} %fusion.8) | data formatting | bytes 6291456
  107.6 42.4 %collective-permute-done.3 = bf16[1024,768]{0,1:T(8,128)(2,1)} collective-permute-done((bf16[1024,768]{0,1:T(8,128)(2,1)}, bf16[1024,768]{0,1:T(8,128)(2,1)}, u32[]{:S(2)}, u32[]{:S(2)}) %collective-permute-start.3) | collective-permute-done | bytes 1572896 | tf_op jit(solution)/shard_map/ppermute | solution.py:9
  150.1 5.5 %collective-permute-done.2 = bf16[1024,768]{0,1:T(8,128)(2,1)} collective-permute-done((bf16[1024,768]{0,1:T(8,128)(2,1)}, bf16[1024,768]{0,1:T(8,128)(2,1)}, u32[]{:S(2)}, u32[]{:S(2)}) %collective-permute-start.2) | collective-permute-done | bytes 1572896 | tf_op jit(solution)/shard_map/ppermute | solution.py:9
  155.6 4.7 %fusion.10 = (f32[1024]{0:T(1024)S(1)}, f32[1024,768]{0,1:T(8,128)S(1)}) fusion(bf16[1024,768]{0,1:T(8,128)(2,1)S(1)} %copy.8, f32[1024]{0:T(1024)S(1)} %add_rsqrt_fusion, bf16[1024,768]{0,1:T(8,128)(2,1)} %collective-permute-done.3, bf16[1024,768]{0,1:T(8,128)(2,1)} %collective-permute-done.2, bf16[1024,1024]{1,0:T(8,128)(2,1)} %copy-done.1, ...), kind=kOutput, calls=%fused_computation.18 | convolution fusion | flops 1619262464 | bytes 11546624 | tf_op jit(solution)/shard_map/dot_general | solution.py:37
  160.2 4.5 %fusion.12 = f32[1024,768]{0,1:T(8,128)} fusion(bf16[1024,768]{0,1:T(8,128)(2,1)S(1)} %copy.8, f32[1024]{0:T(1024)S(1)} %get-tuple-element.6, f32[1024]{0:T(1024)S(1)} %add_rsqrt_fusion, bf16[1024,768]{0,1:T(8,128)(2,1)} %collective-permute-done.3, f32[1024,768]{0,1:T(8,128)S(1)} %get-tuple-element.7, bf16[1024,768]{0,1:T(8,128)(2,1)} %collective-permute-done.2), kind=kLoop, calls=%fused_computation.20 | loop fusion | flops 7077888 | bytes 11018240 | tf_op jit(solution)/shard_map/mul | solution.py:33
  164.7 3.5 %copy.12 = f32[1024,768]{1,0:T(8,128)} copy(f32[1024,768]{0,1:T(8,128)} %fusion.12) | data formatting | bytes 6291456
  (2 shorter events, 0.0 us)
Async XLA Ops:
  4.3 9.8 %copy-start = (s32[1,1024]{1,0:T(1,128)S(1)}, s32[1,1024]{1,0:T(1,128)}, u32[]{:S(2)}) copy-start(s32[1,1024]{1,0:T(1,128)} %param.7) | copy-start | bytes 12292
  4.3 71.4 %collective-permute-start.1 = (bf16[1024,768]{0,1:T(8,128)(2,1)}, bf16[1024,768]{0,1:T(8,128)(2,1)}, u32[]{:S(2)}, u32[]{:S(2)}) collective-permute-start(bf16[1024,768]{0,1:T(8,128)(2,1)} %fusion.2), channel_id=1, source_target_pairs={{0,31},{1,0},{2,1},{3,2},{4,3},{5,4},{6,5},{7,6},{8,7},{9,8},{10,9... | collective-permute-start | bytes 4718600 | tf_op jit(solution)/shard_map/ppermute | solution.py:9
  10.6 72.0 %collective-permute-start = (bf16[1024,768]{0,1:T(8,128)(2,1)}, bf16[1024,768]{0,1:T(8,128)(2,1)}, u32[]{:S(2)}, u32[]{:S(2)}) collective-permute-start(bf16[1024,768]{0,1:T(8,128)(2,1)} %fusion.2), channel_id=1, source_target_pairs={{0,1},{1,2},{2,3},{3,4},{4,5},{5,6},{6,7},{7,8},{8,9},{9,10},{10,1... | collective-permute-start | bytes 4718600 | tf_op jit(solution)/shard_map/ppermute | solution.py:9
  19.0 4.0 %copy-start.1 = (bf16[1024,1024]{1,0:T(8,128)(2,1)}, bf16[1024,1024]{1,0:T(8,128)(2,1)S(1)}, u32[]{:S(2)}) copy-start(bf16[1024,1024]{1,0:T(8,128)(2,1)S(1)} %multiply_convert_fusion.2) | copy-start | bytes 6291460
  82.7 67.4 %collective-permute-start.3 = (bf16[1024,768]{0,1:T(8,128)(2,1)}, bf16[1024,768]{0,1:T(8,128)(2,1)}, u32[]{:S(2)}, u32[]{:S(2)}) collective-permute-start(bf16[1024,768]{0,1:T(8,128)(2,1)} %convolution_convert_fusion), channel_id=1, source_target_pairs={{0,1},{1,2},{2,3},{3,4},{4,5},{5,6},{6,7},{7,8},{8,9},{9,10},{10,1... | collective-permute-start | bytes 4718600 | tf_op jit(solution)/shard_map/ppermute | solution.py:9
  89.6 65.9 %collective-permute-start.2 = (bf16[1024,768]{0,1:T(8,128)(2,1)}, bf16[1024,768]{0,1:T(8,128)(2,1)}, u32[]{:S(2)}, u32[]{:S(2)}) collective-permute-start(bf16[1024,768]{0,1:T(8,128)(2,1)} %convolution_convert_fusion.1), channel_id=1, source_target_pairs={{0,31},{1,0},{2,1},{3,2},{4,3},{5,4},{6,5},{7,6},{8,7},{9,8},{10,9... | collective-permute-start | bytes 4718600 | tf_op jit(solution)/shard_map/ppermute | solution.py:9
where the time goes:
time: 169 us; the launch traced here: 168 us
  waiting for transfers between devices  101 us (60%)
  matrix products  34.3 us (20%)
  starting transfers between devices  11.7 us (7%)
  local copies, waits for them, and re-layouts  10.5 us (6%)
  other arithmetic  9.07 us (5%)
  between operations  2.08 us (1%)
    ppermute x4, waiting for transfers between devices, passed_along(): lax.ppermute(x, axis, [(i, (i + by) % devices) for i in range(devices)])  101 us
    dot_general x6, matrix products, similarity_entries(): return jnp.dot(left, right, preferred_element_type=jnp.float32)  21.5 us
    dot_general x3, matrix products, gradient_panel(): jnp.dot(picture_rows, caption_rows.T, preferred_element_type=jnp.float32)  12.8 us
    ppermute x4, starting transfers between devices, passed_along(): lax.ppermute(x, axis, [(i, (i + by) % devices) for i in range(devices)])  11.7 us
    unnamed x8, local copies, waits for them, and re-layouts  10.5 us
    mul x2, other arithmetic, unit_backward(): inverse_norm * (grad - unit * jnp.sum(unit * grad, -1, keepdims=True))  6.78 us
  transfers between devices with their start and end apart: 4, of which 3 were waited for; matrix products, arithmetic and copies ran while one was open for 22% of the time, Pallas kernels for 0%

commit v1 on v0

v1 whole, which is shorter than its diff:
```python
import functools

import jax
import jax.numpy as jnp
from jax import lax
from jax.experimental import pallas as pl
from jax.experimental.pallas import tpu as pltpu
from jax.sharding import PartitionSpec as P

LOG2E = 1.4426950408889634
CHUNK = 128
TILE = 512
AHEAD = 2
LAG = 2


def rows_at(index, size):
    return pl.ds(pl.multiple_of(index * size, size), size)


def weights(scores, scale, shift, top):
    return top / (1.0 + jnp.exp2(scale * scores + shift))


def dot_t(left, right):
    return lax.dot_general(left, right, (((1,), (1,)), ((), ())), preferred_element_type=jnp.float32)


def kernel(
    sizes, image_ref, text_ref, pair_ref, exponent_ref, offset_ref, image_out, text_out,
    unit, norm, near, far, send_sem, near_sem, pass_sem, far_sem,
):
    ring, inner, rows, chunk, tile = sizes
    steps = rows // chunk
    me = lax.axis_index("grp") * inner + lax.axis_index("dp")
    odd = lax.rem(me, 2)
    partner = me + 1 - 2 * odd
    onward = lax.rem(me + 2 - 4 * odd + ring, ring)
    behind = lax.rem(me - 2 + 4 * odd + ring, ring)

    def place(index):
        return (index // inner, lax.rem(index, inner))

    barrier = pltpu.get_barrier_semaphore()
    for other in (partner, onward, behind):
        pl.semaphore_signal(barrier, inc=1, device_id=place(other), device_id_type=pl.DeviceIdType.MESH)
    pl.semaphore_wait(barrier, 3)

    def own_copy(kind, j):
        return pltpu.make_async_remote_copy(
            src_ref=unit.at[kind, rows_at(j, chunk)],
            dst_ref=near.at[kind, rows_at(j, chunk)],
            send_sem=send_sem.at[kind, j],
            recv_sem=near_sem.at[kind, j],
            device_id=place(partner),
            device_id_type=pl.DeviceIdType.MESH,
        )

    def pass_copy(kind, j):
        return pltpu.make_async_remote_copy(
            src_ref=near.at[kind, rows_at(j, chunk)],
            dst_ref=far.at[kind, rows_at(j, chunk)],
            send_sem=pass_sem.at[kind, j],
            recv_sem=far_sem.at[kind, j],
            device_id=place(onward),
            device_id_type=pl.DeviceIdType.MESH,
        )

    raws = (text_ref, image_ref)
    outs = (text_out, image_out)

    @pl.loop(0, steps)
    def _(j):
        at = rows_at(j, chunk)
        for kind in range(2):
            values = raws[kind][at, :].astype(jnp.float32)
            inverse = lax.rsqrt(jnp.sum(values * values, -1, keepdims=True) + 1e-06)
            norm[kind, at, :] = inverse
            unit[kind, at, :] = (values * inverse).astype(jnp.bfloat16)
            outs[kind][at, :] = jnp.zeros_like(values)

            @pl.when(j < AHEAD)
            def _():
                own_copy(kind, j).start()

    top = jnp.exp(jnp.full((1, chunk), exponent_ref[0], jnp.float32))
    scale = top * -LOG2E
    shift = jnp.full((1, chunk), offset_ref[0], jnp.float32) * -LOG2E

    def spread(kind, block):
        out = outs[1 - kind]

        @pl.loop(0, rows // tile)
        def _(r):
            at = rows_at(r, tile)
            panel = weights(dot_t(unit[1 - kind, at, :], block), scale, shift, top)
            out[at, :] += jnp.dot(panel.astype(jnp.bfloat16), block, preferred_element_type=jnp.float32)

    def own_block(j):
        chunk_at = rows_at(j, chunk)
        block = unit[1, chunk_at, :]
        match = pair_ref[:, chunk_at]

        @pl.loop(0, rows // tile)
        def _(r):
            at = rows_at(r, tile)
            captions = unit[0, at, :]
            hit = match == lax.broadcasted_iota(jnp.int32, (tile, chunk), 0) + r * tile
            scores = dot_t(captions, block)
            power = scale * scores + shift
            panel = top / (1.0 + jnp.exp2(jnp.where(hit, -power, power)))
            panel = jnp.where(hit, -panel, panel).astype(jnp.bfloat16)
            text_out[at, :] += jnp.dot(panel, block, preferred_element_type=jnp.float32)
            image_out[chunk_at, :] += lax.dot_general(
                panel, captions, (((0,), (0,)), ((), ())), preferred_element_type=jnp.float32
            )

    @pl.loop(0, steps + LAG)
    def _(j):
        @pl.when(j < steps)
        def _():
            own_block(j)
            for kind in range(2):
                own_copy(kind, j).wait_recv()
                pass_copy(kind, j).start()

                @pl.when(j + AHEAD < steps)
                def _():
                    own_copy(kind, j + AHEAD).start()

            for kind in range(2):
                spread(kind, near[kind, rows_at(j, chunk), :])

        @pl.when(j >= LAG)
        def _():
            for kind in range(2):
                pass_copy(kind, j - LAG).wait_recv()
                spread(kind, far[kind, rows_at(j - LAG, chunk), :])

    @pl.loop(0, steps)
    def _(j):
        at = rows_at(j, chunk)
        for kind in range(2):
            inverse = norm[kind, at, :]
            values = raws[kind][at, :].astype(jnp.float32) * inverse
            grad = outs[kind][at, :]
            outs[kind][at, :] = inverse * (grad - values * jnp.sum(values * grad, -1, keepdims=True))
            own_copy(kind, j).wait_send()
            pass_copy(kind, j).wait_send()


def local(ring, inner, photo, sentence, companion, exponent, offset):
    rows, width = photo.shape
    steps = rows // CHUNK
    vmem = pl.BlockSpec(memory_space=pltpu.VMEM)
    smem = pl.BlockSpec(memory_space=pltpu.SMEM)
    grad = jax.ShapeDtypeStruct((rows, width), jnp.float32)
    return pl.pallas_call(
        functools.partial(kernel, (ring, inner, rows, CHUNK, TILE)),
        out_shape=(grad, grad),
        in_specs=[vmem, vmem, vmem, smem, smem],
        out_specs=(vmem, vmem),
        scratch_shapes=[
            pltpu.VMEM((2, rows, width), jnp.bfloat16),
            pltpu.VMEM((2, rows, 1), jnp.float32),
            pltpu.VMEM((2, rows, width), jnp.bfloat16),
            pltpu.VMEM((2, rows, width), jnp.bfloat16),
            pltpu.SemaphoreType.DMA((2, steps)),
            pltpu.SemaphoreType.DMA((2, steps)),
            pltpu.SemaphoreType.DMA((2, steps)),
            pltpu.SemaphoreType.DMA((2, steps)),
        ],
        compiler_params=pltpu.CompilerParams(
            collective_id=0, has_side_effects=True, vmem_limit_bytes=48 * 1024 * 1024
        ),
        cost_estimate=pl.CostEstimate(
            flops=22 * rows * rows * width, bytes_accessed=12 * rows * width, transcendentals=10 * rows * rows
        ),
    )(photo, sentence, companion, exponent, offset)


def solution(mesh):
    inner = mesh.shape["dp"]
    ring = mesh.shape["grp"] * inner
    placed = (P(("grp", "dp"), None), P(("grp", "dp"), None), P(("grp", "dp"), None), P(), P())
    return jax.shard_map(
        functools.partial(local, ring, inner),
        mesh=mesh,
        in_specs=placed,
        out_specs=(P(("grp", "dp"), None), P(("grp", "dp"), None)),
        check_vma=False,
    )
```

time: 169 us -> 116 us (0.69)
  Pallas kernels: 0 us -> 105 us
  waiting for transfers between devices: 101 us -> 0 us
  matrix products: 34.3 us -> 0 us
  starting transfers between devices: 11.7 us -> 0 us
  other arithmetic: 9.07 us -> 0 us
    pallas_call x0 -> x1, Pallas kernels: none -> 105 us  [local(): pl.pallas_call(functools.partial(kernel, (ring, inner, rows, CHUNK, TILE)...]
    ppermute x4 -> x0, waiting for transfers between devices: 101 us -> none  [passed_along(): lax.ppermute(x, axis, [(i, (i + by) % devices) for i in range(devices)])]
    dot_general x9 -> x0, matrix products: 34.3 us -> none  [the longest x6 21.5 us: similarity_entries(): return jnp.dot(left, right, preferred_element_type=jnp.float32)]
    ppermute x4 -> x0, starting transfers between devices: 11.7 us -> none  [passed_along(): lax.ppermute(x, axis, [(i, (i + by) % devices) for i in range(devices)])]
    mul x2 -> x0, other arithmetic: 6.78 us -> none  [unit_backward(): inverse_norm * (grad - unit * jnp.sum(unit * grad, -1, keepdims=True))]
    unnamed x8 -> x10, local copies, waits for them, and re-layouts: 10.5 us -> 9.07 us
  transfers between devices with their start and end apart: 4 -> 0, of which waited for: 3 -> 0; matrix products, arithmetic and copies ran while one was open for 22% -> 0% of each run, Pallas kernels for 0% -> 0%
where the time goes in v1:
time: 116 us
  Pallas kernels  105 us (91%)
  local copies, waits for them, and re-layouts  9.07 us (8%)
  between operations  1.95 us (2%)
    pallas_call x1, Pallas kernels, local(): pl.pallas_call(functools.partial(kernel, (ring, inner, rows, CHUNK, TILE)...  105 us
    unnamed x10, local copies, waits for them, and re-layouts  9.07 us

profile of v1, /device:TPU:0, one launch (start us, length us, event | category | flops | bytes accessed | tf_op | source)
XLA Modules:
  0.0 116.0 jit_solution(12669355944202890750)
XLA Ops:
  1.9 0.0 copy-start
  1.9 1.4 %copy-done = bf16[1024,768]{1,0:T(8,128)(2,1)S(1)} copy-done((bf16[1024,768]{1,0:T(8,128)(2,1)S(1)}, bf16[1024,768]{1,0:T(8,128)(2,1)}, u32[]{:S(2)}) %copy-start) | copy-done | bytes 1572888
  3.3 0.0 copy-start.1
  3.3 1.4 %copy-done.1 = bf16[1024,768]{1,0:T(8,128)(2,1)S(1)} copy-done((bf16[1024,768]{1,0:T(8,128)(2,1)S(1)}, bf16[1024,768]{1,0:T(8,128)(2,1)}, u32[]{:S(2)}) %copy-start.1) | copy-done | bytes 1572888
  4.7 0.0 copy-start.2
  4.7 0.7 copy-done.2
  5.4 105.0 %shard_map.68 = (f32[1024,768]{1,0:T(8,128)}, f32[1024,768]{1,0:T(8,128)}) custom-call(bf16[1024,768]{1,0:T(8,128)(2,1)S(1)} %copy-done, bf16[1024,768]{1,0:T(8,128)(2,1)S(1)} %copy-done.1, s32[1,1024]{1,0:T(1,128)S(1)} %copy-done.2, f32[1]{0:T(128)S(6)} %copy.9.exponent_ref, f32[1]{0:T(128)S(6)} %copy.10.offset_ref), custom_call_target="tpu_custom_call" | custom-call | flops 17716740096 | bytes 9437184 | tf_op jit(solution)/shard_map/pallas_call | solution.py:158
  110.5 0.0 copy-start.3
  110.5 3.9 %copy.11 = f32[1024,768]{1,0:T(8,128)} copy(f32[1024,768]{1,0:T(8,128)} %get-tuple-element.4) | data formatting | bytes 6291456
  114.4 0.0 copy-done.3
  114.4 1.7 %copy.12 = f32[1024,768]{1,0:T(8,128)} copy(f32[1024,768]{1,0:T(8,128)S(1)} %copy-done.3) | data formatting | bytes 6291456
Async XLA Ops:
  1.9 1.4 %copy-start = (bf16[1024,768]{1,0:T(8,128)(2,1)S(1)}, bf16[1024,768]{1,0:T(8,128)(2,1)}, u32[]{:S(2)}) copy-start(bf16[1024,768]{1,0:T(8,128)(2,1)} %image_ref.1) | copy-start | bytes 4718596
  3.3 1.4 %copy-start.1 = (bf16[1024,768]{1,0:T(8,128)(2,1)S(1)}, bf16[1024,768]{1,0:T(8,128)(2,1)}, u32[]{:S(2)}) copy-start(bf16[1024,768]{1,0:T(8,128)(2,1)} %text_ref.1) | copy-start | bytes 4718596
  4.7 0.7 copy-start.2
  110.5 3.9 %copy-start.3 = (f32[1024,768]{1,0:T(8,128)S(1)}, f32[1024,768]{1,0:T(8,128)}, u32[]{:S(2)}) copy-start(f32[1024,768]{1,0:T(8,128)} %get-tuple-element.5) | copy-start | bytes 9437188

commit v2 on v1

v2 whole, which is shorter than its diff:
```python
import functools

import jax
import jax.numpy as jnp
from jax import lax
from jax.experimental import pallas as pl
from jax.experimental.pallas import tpu as pltpu
from jax.sharding import PartitionSpec as P

LOG2E = 1.4426950408889634
SUB = 128
UNIT = 256
TILE = 256
AHEAD = 2


def rows_at(index, size):
    return pl.ds(pl.multiple_of(index * size, size), size)


def dot_t(left, right):
    return lax.dot_general(left, right, (((1,), (1,)), ((), ())), preferred_element_type=jnp.float32)


def kernel(
    sizes, text_ref, image_ref, pair_ref, exponent_ref, offset_ref, total,
    raw, pairs, unit, near, far, load_sem, pair_sem, send_sem, near_sem, pass_sem, far_sem,
):
    ring, inner, rows = sizes
    subs = rows // SUB
    units = 2 * (rows // UNIT)
    parts = UNIT // SUB
    me = lax.axis_index("grp") * inner + lax.axis_index("dp")
    odd = lax.rem(me, 2)
    partner = me + 1 - 2 * odd
    onward = lax.rem(me + 2 - 4 * odd + ring, ring)
    behind = lax.rem(me - 2 + 4 * odd + ring, ring)
    sources = (text_ref, image_ref)

    def place(index):
        return (index // inner, lax.rem(index, inner))

    def load(kind, j):
        return pltpu.make_async_copy(
            sources[kind].at[rows_at(j, UNIT)], raw.at[kind, rows_at(j, UNIT)], load_sem.at[kind, j]
        )

    for j in range(rows // UNIT):
        for kind in range(2):
            load(kind, j).start()
    load_pairs = pltpu.make_async_copy(pair_ref, pairs, pair_sem)
    load_pairs.start()

    barrier = pltpu.get_barrier_semaphore()
    for other in (partner, onward, behind):
        pl.semaphore_signal(barrier, inc=1, device_id=place(other), device_id_type=pl.DeviceIdType.MESH)
    pl.semaphore_wait(barrier, 3)

    def own_copy(kind, s):
        return pltpu.make_async_remote_copy(
            src_ref=unit.at[kind, rows_at(s, SUB)],
            dst_ref=near.at[kind, rows_at(s, SUB)],
            send_sem=send_sem.at[kind, s],
            recv_sem=near_sem.at[kind, s],
            device_id=place(partner),
            device_id_type=pl.DeviceIdType.MESH,
        )

    def pass_copy(kind, s):
        return pltpu.make_async_remote_copy(
            src_ref=near.at[kind, rows_at(s, SUB)],
            dst_ref=far.at[kind, rows_at(s, SUB)],
            send_sem=pass_sem.at[kind, s],
            recv_sem=far_sem.at[kind, s],
            device_id=place(onward),
            device_id_type=pl.DeviceIdType.MESH,
        )

    @pl.loop(0, rows // UNIT)
    def _(j):
        for kind in range(2):
            load(kind, j).wait()
            for part in range(parts):
                s = j * parts + part
                at = rows_at(s, SUB)
                values = raw[kind, at, :].astype(jnp.float32)
                inverse = lax.rsqrt(jnp.sum(values * values, -1, keepdims=True) + 1e-06)
                unit[kind, at, :] = (values * inverse).astype(jnp.bfloat16)

                @pl.when(j * 2 + kind < AHEAD)
                def _():
                    own_copy(kind, s).start()

    load_pairs.wait()
    top = jnp.exp(jnp.full((1, UNIT), exponent_ref[0], jnp.float32))
    scale = top * -LOG2E
    shift = jnp.full((1, UNIT), offset_ref[0], jnp.float32) * -LOG2E

    def spread(kind, block):
        for r in range(rows // TILE):
            at = pl.ds(r * TILE, TILE)
            power = scale * dot_t(unit[1 - kind, at, :], block) + shift
            panel = (top / (1.0 + jnp.exp2(power))).astype(jnp.bfloat16)
            total[1 - kind, at, :] += jnp.dot(panel, block, preferred_element_type=jnp.float32)

    def own_block(j):
        block_at = rows_at(j, UNIT)
        block = unit[1, block_at, :]
        match = pairs[:, block_at]
        for r in range(rows // TILE):
            at = pl.ds(r * TILE, TILE)
            captions = unit[0, at, :]
            hit = match == lax.broadcasted_iota(jnp.int32, (TILE, UNIT), 0) + r * TILE
            power = scale * dot_t(captions, block) + shift
            panel = top / (1.0 + jnp.exp2(jnp.where(hit, -power, power)))
            panel = jnp.where(hit, -panel, panel).astype(jnp.bfloat16)
            text_term = jnp.dot(panel, block, preferred_element_type=jnp.float32)
            image_term = lax.dot_general(
                panel, captions, (((0,), (0,)), ((), ())), preferred_element_type=jnp.float32
            )

            @pl.when(j == 0)
            def _():
                total[0, at, :] = text_term

            @pl.when(j > 0)
            def _():
                total[0, at, :] += text_term

            if r == 0:
                total[1, block_at, :] = image_term
            else:
                total[1, block_at, :] += image_term

    @pl.loop(0, rows // UNIT)
    def _(j):
        own_block(j)

    @pl.loop(0, units + 1)
    def _(u):
        @pl.when(u < units)
        def _():
            kind, j = lax.rem(u, 2), u // 2
            for part in range(parts):
                s = j * parts + part
                own_copy(kind, s).wait_recv()
                pass_copy(kind, s).start()

                @pl.when(u + AHEAD < units)
                def _():
                    later = u + AHEAD
                    own_copy(lax.rem(later, 2), (later // 2) * parts + part).start()

            spread(kind, near[kind, rows_at(j, UNIT), :])

        @pl.when(u > 0)
        def _():
            kind, j = lax.rem(u - 1, 2), (u - 1) // 2
            for part in range(parts):
                pass_copy(kind, j * parts + part).wait_recv()
            spread(kind, far[kind, rows_at(j, UNIT), :])

    @pl.loop(0, subs)
    def _(s):
        for kind in range(2):
            own_copy(kind, s).wait_send()
            pass_copy(kind, s).wait_send()


def backward_kernel(total, text_ref, image_ref, text_out, image_out):
    for kind, (ref, out) in enumerate(((text_ref, text_out), (image_ref, image_out))):
        values = ref[...].astype(jnp.float32)
        inverse = lax.rsqrt(jnp.sum(values * values, -1, keepdims=True) + 1e-06)
        values = values * inverse
        grad = total[kind]
        out[...] = inverse * (grad - values * jnp.sum(values * grad, -1, keepdims=True))


def local(ring, inner, photo, sentence, companion, exponent, offset):
    rows, width = photo.shape
    subs = rows // SUB
    anywhere = pl.BlockSpec(memory_space=pltpu.HBM)
    vmem = pl.BlockSpec(memory_space=pltpu.VMEM)
    smem = pl.BlockSpec(memory_space=pltpu.SMEM)
    blocks = pltpu.VMEM((2, rows, width), jnp.bfloat16)
    total = pl.pallas_call(
        functools.partial(kernel, (ring, inner, rows)),
        out_shape=jax.ShapeDtypeStruct((2, rows, width), jnp.float32),
        in_specs=[anywhere, anywhere, anywhere, smem, smem],
        out_specs=vmem,
        scratch_shapes=[
            blocks,
            pltpu.VMEM((1, rows), jnp.int32),
            blocks,
            blocks,
            blocks,
            pltpu.SemaphoreType.DMA((2, rows // UNIT)),
            pltpu.SemaphoreType.DMA,
            pltpu.SemaphoreType.DMA((2, subs)),
            pltpu.SemaphoreType.DMA((2, subs)),
            pltpu.SemaphoreType.DMA((2, subs)),
            pltpu.SemaphoreType.DMA((2, subs)),
        ],
        compiler_params=pltpu.CompilerParams(
            collective_id=0, has_side_effects=True, vmem_limit_bytes=40 * 1024 * 1024
        ),
        cost_estimate=pl.CostEstimate(
            flops=22 * rows * rows * width, bytes_accessed=12 * rows * width, transcendentals=10 * rows * rows
        ),
    )(sentence, photo, companion, exponent, offset)
    tile = 256
    row_block = pl.BlockSpec((tile, width), lambda i: (i, 0))
    grad = jax.ShapeDtypeStruct((rows, width), jnp.float32)
    text_grad, image_grad = pl.pallas_call(
        backward_kernel,
        grid=(rows // tile,),
        out_shape=(grad, grad),
        in_specs=[pl.BlockSpec((2, tile, width), lambda i: (0, i, 0)), row_block, row_block],
        out_specs=(row_block, row_block),
        compiler_params=pltpu.CompilerParams(vmem_limit_bytes=24 * 1024 * 1024),
        cost_estimate=pl.CostEstimate(
            flops=20 * rows * width, bytes_accessed=20 * rows * width, transcendentals=0
        ),
    )(total, sentence, photo)
    return image_grad, text_grad


def solution(mesh):
    inner = mesh.shape["dp"]
    ring = mesh.shape["grp"] * inner
    placed = (P(("grp", "dp"), None), P(("grp", "dp"), None), P(("grp", "dp"), None), P(), P())
    return jax.shard_map(
        functools.partial(local, ring, inner),
        mesh=mesh,
        in_specs=placed,
        out_specs=(P(("grp", "dp"), None), P(("grp", "dp"), None)),
        check_vma=False,
    )
```

time: 116 us -> 105 us (0.905)
  Pallas kernels: 105 us -> 98.9 us
  local copies, waits for them, and re-layouts: 9.07 us -> 3.49 us
    pallas_call x1 -> x2, Pallas kernels: 105 us -> 98.9 us  [the longest x1 95 us: local(): pl.pallas_call(functools.partial(kernel, (ring, inner, rows)), out_shape=...]
    unnamed x10 -> x6, local copies, waits for them, and re-layouts: 9.07 us -> 3.49 us
where the time goes in v2:
time: 105 us; the launch traced here: 104 us
  Pallas kernels  98.9 us (94%)
  local copies, waits for them, and re-layouts  3.49 us (3%)
  between operations  1.94 us (2%)
    pallas_call x1, Pallas kernels, local(): pl.pallas_call(functools.partial(kernel, (ring, inner, rows)), out_shape=...  95 us
    pallas_call x1, Pallas kernels, local(): pl.pallas_call(backward_kernel, grid=(rows // tile,), out_shape=(grad, gr...  3.94 us
    unnamed x6, local copies, waits for them, and re-layouts  3.49 us

profile of v2, /device:TPU:0, one launch (start us, length us, event | category | flops | bytes accessed | tf_op | source)
XLA Modules:
  0.0 104.4 jit_solution(10309333956167640910)
XLA Ops:
  1.9 0.0 copy-start
  1.9 1.4 %copy-done = bf16[1024,768]{1,0:T(8,128)(2,1)S(1)} copy-done((bf16[1024,768]{1,0:T(8,128)(2,1)S(1)}, bf16[1024,768]{1,0:T(8,128)(2,1)}, u32[]{:S(2)}) %copy-start) | copy-done | bytes 1572888
  3.3 0.0 copy-start.1
  3.3 1.4 %copy-done.1 = bf16[1024,768]{1,0:T(8,128)(2,1)S(1)} copy-done((bf16[1024,768]{1,0:T(8,128)(2,1)S(1)}, bf16[1024,768]{1,0:T(8,128)(2,1)}, u32[]{:S(2)}) %copy-start.1) | copy-done | bytes 1572888
  4.7 0.0 copy-start.2
  4.7 0.7 copy-done.2
  5.4 95.0 %shard_map.68.total = f32[2,1024,768]{2,1,0:T(8,128)S(1)} custom-call(bf16[1024,768]{1,0:T(8,128)(2,1)S(1)} %copy-done, bf16[1024,768]{1,0:T(8,128)(2,1)S(1)} %copy-done.1, s32[1,1024]{1,0:T(1,128)S(1)} %copy-done.2, f32[1]{0:T(128)S(6)} %copy.7.exponent_ref, f32[1]{0:T(128)S(6)} %copy.8.offset_ref), custom_call_target="tpu_custom_call" | custom-call | flops 17716740096 | bytes 9437184 | tf_op jit(solution)/shard_map/pallas_call | solution.py:186
  100.4 3.9 %shard_map.69 = (f32[1024,768]{1,0:T(8,128)}, f32[1024,768]{1,0:T(8,128)}) custom-call(f32[2,1024,768]{2,1,0:T(8,128)S(1)} %shard_map.68.total, bf16[1024,768]{1,0:T(8,128)(2,1)S(1)} %copy-done, bf16[1024,768]{1,0:T(8,128)(2,1)S(1)} %copy-done.1), custom_call_target="tpu_custom_call" | custom-call | flops 15728640 | bytes 15728640 | tf_op jit(solution)/shard_map/pallas_call | solution.py:214
Async XLA Ops:
  1.9 1.4 %copy-start = (bf16[1024,768]{1,0:T(8,128)(2,1)S(1)}, bf16[1024,768]{1,0:T(8,128)(2,1)}, u32[]{:S(2)}) copy-start(bf16[1024,768]{1,0:T(8,128)(2,1)} %text_ref.3) | copy-start | bytes 4718596
  3.3 1.4 %copy-start.1 = (bf16[1024,768]{1,0:T(8,128)(2,1)S(1)}, bf16[1024,768]{1,0:T(8,128)(2,1)}, u32[]{:S(2)}) copy-start(bf16[1024,768]{1,0:T(8,128)(2,1)} %image_ref.3) | copy-start | bytes 4718596
  4.7 0.7 copy-start.2

commit v3 on v2

--- a/solution.py
+++ b/solution.py
@@ -11,7 +11,8 @@
 SUB = 128
 UNIT = 256
 TILE = 256
-AHEAD = 2
+AHEAD = 6
+LAG = 4
 
 
 def rows_at(index, size):
@@ -28,7 +29,6 @@
 ):
     ring, inner, rows = sizes
     subs = rows // SUB
-    units = 2 * (rows // UNIT)
     parts = UNIT // SUB
     me = lax.axis_index("grp") * inner + lax.axis_index("dp")
     odd = lax.rem(me, 2)
@@ -86,8 +86,9 @@
                 values = raw[kind, at, :].astype(jnp.float32)
                 inverse = lax.rsqrt(jnp.sum(values * values, -1, keepdims=True) + 1e-06)
                 unit[kind, at, :] = (values * inverse).astype(jnp.bfloat16)
-
-                @pl.when(j * 2 + kind < AHEAD)
+                total[kind, at, :] = jnp.zeros_like(values)
+
+                @pl.when((j * 2 + kind) * parts + part < AHEAD)
                 def _():
                     own_copy(kind, s).start()
 
@@ -119,46 +120,46 @@
                 panel, captions, (((0,), (0,)), ((), ())), preferred_element_type=jnp.float32
             )
 
-            @pl.when(j == 0)
+            total[0, at, :] += text_term
+            total[1, block_at, :] += image_term
+
+    def place_of(v):
+        return lax.rem(v // parts, 2), (v // (2 * parts)) * parts + lax.rem(v, parts)
+
+    own_block(0)
+
+    @pl.loop(0, 2 * subs + LAG - 1)
+    def _(v):
+        @pl.when(v < 2 * subs)
+        def _():
+            kind, s = place_of(v)
+            own_copy(kind, s).wait_recv()
+            pass_copy(kind, s).start()
+
+            @pl.when(v + AHEAD < 2 * subs)
             def _():
-                total[0, at, :] = text_term
-
-            @pl.when(j > 0)
+                own_copy(*place_of(v + AHEAD)).start()
+
+        u = v // parts
+
+        @pl.when(lax.rem(v, parts) == 0)
+        def _():
+            @pl.when(u + 1 < rows // UNIT)
             def _():
-                total[0, at, :] += text_term
-
-            if r == 0:
-                total[1, block_at, :] = image_term
-            else:
-                total[1, block_at, :] += image_term
-
-    @pl.loop(0, rows // UNIT)
-    def _(j):
-        own_block(j)
-
-    @pl.loop(0, units + 1)
-    def _(u):
-        @pl.when(u < units)
+                own_block(u + 1)
+
+            @pl.when(v >= LAG)
+            def _():
+                w = u - LAG // parts
+                kind, j = lax.rem(w, 2), w // 2
+                for part in range(parts):
+                    pass_copy(kind, j * parts + part).wait_recv()
+                spread(kind, far[kind, rows_at(j, UNIT), :])
+
+        @pl.when((lax.rem(v, parts) == parts - 1) & (v < 2 * subs))
         def _():
             kind, j = lax.rem(u, 2), u // 2
-            for part in range(parts):
-                s = j * parts + part
-                own_copy(kind, s).wait_recv()
-                pass_copy(kind, s).start()
-
-                @pl.when(u + AHEAD < units)
-                def _():
-                    later = u + AHEAD
-                    own_copy(lax.rem(later, 2), (later // 2) * parts + part).start()
-
             spread(kind, near[kind, rows_at(j, UNIT), :])
-
-        @pl.when(u > 0)
-        def _():
-            kind, j = lax.rem(u - 1, 2), (u - 1) // 2
-            for part in range(parts):
-                pass_copy(kind, j * parts + part).wait_recv()
-            spread(kind, far[kind, rows_at(j, UNIT), :])
 
     @pl.loop(0, subs)
     def _(s):

time: 105 us -> 94.2 us (0.90)
  Pallas kernels: 98.9 us -> 87.1 us
    pallas_call x1, Pallas kernels: 95 us -> 83.2 us  [local(): pl.pallas_call(functools.partial(kernel, (ring, inner, rows)), out_shape=...]
where the time goes in v3:
time: 94.2 us; the launch traced here: 92.5 us
  Pallas kernels  87.1 us (92%)
  local copies, waits for them, and re-layouts  3.49 us (4%)
  between operations  1.94 us (2%)
    pallas_call x1, Pallas kernels, local(): pl.pallas_call(functools.partial(kernel, (ring, inner, rows)), out_shape=...  83.2 us
    pallas_call x1, Pallas kernels, local(): pl.pallas_call(backward_kernel, grid=(rows // tile,), out_shape=(grad, gr...  3.94 us
    unnamed x6, local copies, waits for them, and re-layouts  3.49 us

profile of v3, /device:TPU:0, one launch (start us, length us, event | category | flops | bytes accessed | tf_op | source)
XLA Modules:
  0.0 92.5 jit_solution(6654730096694695322)
XLA Ops:
  1.9 0.0 copy-start
  1.9 1.4 %copy-done = bf16[1024,768]{1,0:T(8,128)(2,1)S(1)} copy-done((bf16[1024,768]{1,0:T(8,128)(2,1)S(1)}, bf16[1024,768]{1,0:T(8,128)(2,1)}, u32[]{:S(2)}) %copy-start) | copy-done | bytes 1572888
  3.3 0.0 copy-start.1
  3.3 1.4 %copy-done.1 = bf16[1024,768]{1,0:T(8,128)(2,1)S(1)} copy-done((bf16[1024,768]{1,0:T(8,128)(2,1)S(1)}, bf16[1024,768]{1,0:T(8,128)(2,1)}, u32[]{:S(2)}) %copy-start.1) | copy-done | bytes 1572888
  4.7 0.0 copy-start.2
  4.7 0.7 copy-done.2
  5.4 83.2 %shard_map.68.total = f32[2,1024,768]{2,1,0:T(8,128)S(1)} custom-call(bf16[1024,768]{1,0:T(8,128)(2,1)S(1)} %copy-done, bf16[1024,768]{1,0:T(8,128)(2,1)S(1)} %copy-done.1, s32[1,1024]{1,0:T(1,128)S(1)} %copy-done.2, f32[1]{0:T(128)S(6)} %copy.7.exponent_ref, f32[1]{0:T(128)S(6)} %copy.8.offset_ref), custom_call_target="tpu_custom_call" | custom-call | flops 17716740096 | bytes 9437184 | tf_op jit(solution)/shard_map/pallas_call | solution.py:187
  88.6 3.9 %shard_map.69 = (f32[1024,768]{1,0:T(8,128)}, f32[1024,768]{1,0:T(8,128)}) custom-call(f32[2,1024,768]{2,1,0:T(8,128)S(1)} %shard_map.68.total, bf16[1024,768]{1,0:T(8,128)(2,1)S(1)} %copy-done, bf16[1024,768]{1,0:T(8,128)(2,1)S(1)} %copy-done.1), custom_call_target="tpu_custom_call" | custom-call | flops 15728640 | bytes 15728640 | tf_op jit(solution)/shard_map/pallas_call | solution.py:215
Async XLA Ops:
  1.9 1.4 %copy-start = (bf16[1024,768]{1,0:T(8,128)(2,1)S(1)}, bf16[1024,768]{1,0:T(8,128)(2,1)}, u32[]{:S(2)}) copy-start(bf16[1024,768]{1,0:T(8,128)(2,1)} %text_ref.3) | copy-start | bytes 4718596
  3.3 1.4 %copy-start.1 = (bf16[1024,768]{1,0:T(8,128)(2,1)S(1)}, bf16[1024,768]{1,0:T(8,128)(2,1)}, u32[]{:S(2)}) copy-start(bf16[1024,768]{1,0:T(8,128)(2,1)} %image_ref.3) | copy-start | bytes 4718596
  4.7 0.7 copy-start.2

commit v4 on v3

--- a/solution.py
+++ b/solution.py
@@ -8,11 +8,11 @@
 from jax.sharding import PartitionSpec as P
 
 LOG2E = 1.4426950408889634
-SUB = 128
+SUB = 64
 UNIT = 256
 TILE = 256
-AHEAD = 6
-LAG = 4
+AHEAD = 12
+LAG = 6
 
 
 def rows_at(index, size):
@@ -25,7 +25,7 @@
 
 def kernel(
     sizes, text_ref, image_ref, pair_ref, exponent_ref, offset_ref, total,
-    raw, pairs, unit, near, far, load_sem, pair_sem, send_sem, near_sem, pass_sem, far_sem,
+    raw, pairs, norm, unit, near, far, load_sem, pair_sem, send_sem, near_sem, pass_sem, far_sem,
 ):
     ring, inner, rows = sizes
     subs = rows // SUB
@@ -85,6 +85,7 @@
                 at = rows_at(s, SUB)
                 values = raw[kind, at, :].astype(jnp.float32)
                 inverse = lax.rsqrt(jnp.sum(values * values, -1, keepdims=True) + 1e-06)
+                norm[kind, at, :] = inverse
                 unit[kind, at, :] = (values * inverse).astype(jnp.bfloat16)
                 total[kind, at, :] = jnp.zeros_like(values)
 
@@ -128,8 +129,25 @@
 
     own_block(0)
 
-    @pl.loop(0, 2 * subs + LAG - 1)
+    def spread_far(w):
+        kind, j = lax.rem(w, 2), w // 2
+        for part in range(parts):
+            pass_copy(kind, j * parts + part).wait_recv()
+        spread(kind, far[kind, rows_at(j, UNIT), :])
+
+    def finish(kind):
+        @pl.loop(0, rows // UNIT)
+        def _(j):
+            at = rows_at(j, UNIT)
+            inverse = norm[kind, at, :]
+            values = raw[kind, at, :].astype(jnp.float32) * inverse
+            grad = total[kind, at, :]
+            total[kind, at, :] = inverse * (grad - values * jnp.sum(values * grad, -1, keepdims=True))
+
+    @pl.loop(0, 2 * subs + parts)
     def _(v):
+        u = v // parts
+
         @pl.when(v < 2 * subs)
         def _():
             kind, s = place_of(v)
@@ -140,26 +158,24 @@
             def _():
                 own_copy(*place_of(v + AHEAD)).start()
 
-        u = v // parts
-
-        @pl.when(lax.rem(v, parts) == 0)
-        def _():
-            @pl.when(u + 1 < rows // UNIT)
+            @pl.when((lax.rem(v, parts) == 0) & (u + 1 < rows // UNIT))
             def _():
                 own_block(u + 1)
 
-            @pl.when(v >= LAG)
+            @pl.when(lax.rem(v, parts) == parts - 1)
             def _():
-                w = u - LAG // parts
-                kind, j = lax.rem(w, 2), w // 2
-                for part in range(parts):
-                    pass_copy(kind, j * parts + part).wait_recv()
-                spread(kind, far[kind, rows_at(j, UNIT), :])
-
-        @pl.when((lax.rem(v, parts) == parts - 1) & (v < 2 * subs))
+                near_kind, j = lax.rem(u, 2), u // 2
+                spread(near_kind, near[near_kind, rows_at(j, UNIT), :])
+
+        @pl.when(v == 2 * subs)
         def _():
-            kind, j = lax.rem(u, 2), u // 2
-            spread(kind, near[kind, rows_at(j, UNIT), :])
+            finish(1)
+
+        @pl.when((v >= LAG) & (lax.rem(v, parts) == LAG % parts))
+        def _():
+            spread_far((v - LAG) // parts)
+
+    finish(0)
 
     @pl.loop(0, subs)
     def _(s):
@@ -168,19 +184,25 @@
             pass_copy(kind, s).wait_send()
 
 
-def backward_kernel(total, text_ref, image_ref, text_out, image_out):
-    for kind, (ref, out) in enumerate(((text_ref, text_out), (image_ref, image_out))):
-        values = ref[...].astype(jnp.float32)
-        inverse = lax.rsqrt(jnp.sum(values * values, -1, keepdims=True) + 1e-06)
-        values = values * inverse
-        grad = total[kind]
-        out[...] = inverse * (grad - values * jnp.sum(values * grad, -1, keepdims=True))
+def move_kernel(total, text_out, image_out, sems):
+    rows = total.shape[1]
+    copies = [
+        pltpu.make_async_copy(
+            total.at[kind, pl.ds(j * UNIT, UNIT)], out.at[pl.ds(j * UNIT, UNIT)], sems.at[kind, j]
+        )
+        for kind, out in enumerate((text_out, image_out))
+        for j in range(rows // UNIT)
+    ]
+    for copy in copies:
+        copy.start()
+    for copy in copies:
+        copy.wait()
 
 
 def local(ring, inner, photo, sentence, companion, exponent, offset):
     rows, width = photo.shape
     subs = rows // SUB
-    anywhere = pl.BlockSpec(memory_space=pltpu.HBM)
+    anywhere = pl.BlockSpec(memory_space=pl.ANY)
     vmem = pl.BlockSpec(memory_space=pltpu.VMEM)
     smem = pl.BlockSpec(memory_space=pltpu.SMEM)
     blocks = pltpu.VMEM((2, rows, width), jnp.bfloat16)
@@ -192,6 +214,7 @@
         scratch_shapes=[
             blocks,
             pltpu.VMEM((1, rows), jnp.int32),
+            pltpu.VMEM((2, rows, 1), jnp.float32),
             blocks,
             blocks,
             blocks,
@@ -209,20 +232,16 @@
             flops=22 * rows * rows * width, bytes_accessed=12 * rows * width, transcendentals=10 * rows * rows
         ),
     )(sentence, photo, companion, exponent, offset)
-    tile = 256
-    row_block = pl.BlockSpec((tile, width), lambda i: (i, 0))
     grad = jax.ShapeDtypeStruct((rows, width), jnp.float32)
     text_grad, image_grad = pl.pallas_call(
-        backward_kernel,
-        grid=(rows // tile,),
+        move_kernel,
         out_shape=(grad, grad),
-        in_specs=[pl.BlockSpec((2, tile, width), lambda i: (0, i, 0)), row_block, row_block],
-        out_specs=(row_block, row_block),
+        in_specs=[vmem],
+        out_specs=(anywhere, anywhere),
+        scratch_shapes=[pltpu.SemaphoreType.DMA((2, rows // UNIT))],
         compiler_params=pltpu.CompilerParams(vmem_limit_bytes=24 * 1024 * 1024),
-        cost_estimate=pl.CostEstimate(
-            flops=20 * rows * width, bytes_accessed=20 * rows * width, transcendentals=0
-        ),
-    )(total, sentence, photo)
+        cost_estimate=pl.CostEstimate(flops=0, bytes_accessed=16 * rows * width, transcendentals=0),
+    )(total)
     return image_grad, text_grad
 
 

time: 94.2 us -> 94.5 us (level); the launches traced: 92.5 us -> 94.3 us
  Pallas kernels: 87.1 us -> 88.9 us
    pallas_call x1, Pallas kernels: 83.2 us -> 86.1 us  [local(): pl.pallas_call(functools.partial(kernel, (ring, inner, rows)), out_shape=...]
    pallas_call x1, Pallas kernels: 3.94 us -> 2.74 us  [local(): pl.pallas_call(move_kernel, out_shape=(grad, grad), in_specs=[vmem], out_...]
where the time goes in v4:
time: 94.5 us; the launch traced here: 94.3 us
  Pallas kernels  88.9 us (94%)
  local copies, waits for them, and re-layouts  3.49 us (4%)
  between operations  1.94 us (2%)
    pallas_call x1, Pallas kernels, local(): pl.pallas_call(functools.partial(kernel, (ring, inner, rows)), out_shape=...  86.1 us
    unnamed x6, local copies, waits for them, and re-layouts  3.49 us
    pallas_call x1, Pallas kernels, local(): pl.pallas_call(move_kernel, out_shape=(grad, grad), in_specs=[vmem], out_...  2.74 us

profile of v4, /device:TPU:0, one launch (start us, length us, event | category | flops | bytes accessed | tf_op | source)
XLA Modules:
  0.0 94.3 jit_solution(11599581664613316992)
XLA Ops:
  1.9 0.0 copy-start
  1.9 1.4 %copy-done = bf16[1024,768]{1,0:T(8,128)(2,1)S(1)} copy-done((bf16[1024,768]{1,0:T(8,128)(2,1)S(1)}, bf16[1024,768]{1,0:T(8,128)(2,1)}, u32[]{:S(2)}) %copy-start) | copy-done | bytes 1572888
  3.3 0.0 copy-start.1
  3.3 1.4 %copy-done.1 = bf16[1024,768]{1,0:T(8,128)(2,1)S(1)} copy-done((bf16[1024,768]{1,0:T(8,128)(2,1)S(1)}, bf16[1024,768]{1,0:T(8,128)(2,1)}, u32[]{:S(2)}) %copy-start.1) | copy-done | bytes 1572888
  4.7 0.0 copy-start.2
  4.7 0.7 copy-done.2
  5.4 86.1 %shard_map.68.total = f32[2,1024,768]{2,1,0:T(8,128)S(1)} custom-call(bf16[1024,768]{1,0:T(8,128)(2,1)S(1)} %copy-done, bf16[1024,768]{1,0:T(8,128)(2,1)S(1)} %copy-done.1, s32[1,1024]{1,0:T(1,128)S(1)} %copy-done.2, f32[1]{0:T(128)S(6)} %copy.7.exponent_ref, f32[1]{0:T(128)S(6)} %copy.8.offset_ref), custom_call_target="tpu_custom_call" | custom-call | flops 17716740096 | bytes 9437184 | tf_op jit(solution)/shard_map/pallas_call | solution.py:209
  91.6 2.7 %shard_map.69 = (f32[1024,768]{1,0:T(8,128)}, f32[1024,768]{1,0:T(8,128)}) custom-call(f32[2,1024,768]{2,1,0:T(8,128)S(1)} %shard_map.68.total), custom_call_target="tpu_custom_call" | custom-call | bytes 12582912 | tf_op jit(solution)/shard_map/pallas_call | solution.py:236
Async XLA Ops:
  1.9 1.4 %copy-start = (bf16[1024,768]{1,0:T(8,128)(2,1)S(1)}, bf16[1024,768]{1,0:T(8,128)(2,1)}, u32[]{:S(2)}) copy-start(bf16[1024,768]{1,0:T(8,128)(2,1)} %text_ref.1) | copy-start | bytes 4718596
  3.3 1.4 %copy-start.1 = (bf16[1024,768]{1,0:T(8,128)(2,1)S(1)}, bf16[1024,768]{1,0:T(8,128)(2,1)}, u32[]{:S(2)}) copy-start(bf16[1024,768]{1,0:T(8,128)(2,1)} %image_ref.1) | copy-start | bytes 4718596
  4.7 0.7 copy-start.2

commit v5 on v4

--- a/solution.py
+++ b/solution.py
@@ -7,10 +7,9 @@
 from jax.experimental.pallas import tpu as pltpu
 from jax.sharding import PartitionSpec as P
 
-LOG2E = 1.4426950408889634
 SUB = 64
 UNIT = 256
-TILE = 256
+TILE = 512
 AHEAD = 12
 LAG = 6
 
@@ -94,15 +93,14 @@
                     own_copy(kind, s).start()
 
     load_pairs.wait()
-    top = jnp.exp(jnp.full((1, UNIT), exponent_ref[0], jnp.float32))
-    scale = top * -LOG2E
-    shift = jnp.full((1, UNIT), offset_ref[0], jnp.float32) * -LOG2E
+    half = 0.5 * jnp.exp(jnp.full((1, UNIT), exponent_ref[0], jnp.float32))
+    shift = jnp.full((1, UNIT), 0.5 * offset_ref[0], jnp.float32)
 
     def spread(kind, block):
         for r in range(rows // TILE):
             at = pl.ds(r * TILE, TILE)
-            power = scale * dot_t(unit[1 - kind, at, :], block) + shift
-            panel = (top / (1.0 + jnp.exp2(power))).astype(jnp.bfloat16)
+            slope = jnp.tanh(half * dot_t(unit[1 - kind, at, :], block) + shift)
+            panel = (half + half * slope).astype(jnp.bfloat16)
             total[1 - kind, at, :] += jnp.dot(panel, block, preferred_element_type=jnp.float32)
 
     def own_block(j):
@@ -113,9 +111,8 @@
             at = pl.ds(r * TILE, TILE)
             captions = unit[0, at, :]
             hit = match == lax.broadcasted_iota(jnp.int32, (TILE, UNIT), 0) + r * TILE
-            power = scale * dot_t(captions, block) + shift
-            panel = top / (1.0 + jnp.exp2(jnp.where(hit, -power, power)))
-            panel = jnp.where(hit, -panel, panel).astype(jnp.bfloat16)
+            slope = jnp.tanh(half * dot_t(captions, block) + shift)
+            panel = (half * slope + jnp.where(hit, -half, half)).astype(jnp.bfloat16)
             text_term = jnp.dot(panel, block, preferred_element_type=jnp.float32)
             image_term = lax.dot_general(
                 panel, captions, (((0,), (0,)), ((), ())), preferred_element_type=jnp.float32

time: 94.5 us -> 94.1 us (level)
  no operation moved by 1% of the time
where the time goes in v5:
time: 94.1 us; the launch traced here: 93.9 us
  Pallas kernels  88.5 us (94%)
  local copies, waits for them, and re-layouts  3.49 us (4%)
  between operations  1.94 us (2%)
    pallas_call x1, Pallas kernels, local(): pl.pallas_call(functools.partial(kernel, (ring, inner, rows)), out_shape=...  85.7 us
    unnamed x6, local copies, waits for them, and re-layouts  3.49 us
    pallas_call x1, Pallas kernels, local(): pl.pallas_call(move_kernel, out_shape=(grad, grad), in_specs=[vmem], out_...  2.74 us

profile of v5, /device:TPU:0, one launch (start us, length us, event | category | flops | bytes accessed | tf_op | source)
XLA Modules:
  0.0 93.9 jit_solution(2679632161869766971)
XLA Ops:
  1.9 0.0 copy-start
  1.9 1.4 %copy-done = bf16[1024,768]{1,0:T(8,128)(2,1)S(1)} copy-done((bf16[1024,768]{1,0:T(8,128)(2,1)S(1)}, bf16[1024,768]{1,0:T(8,128)(2,1)}, u32[]{:S(2)}) %copy-start) | copy-done | bytes 1572888
  3.3 0.0 copy-start.1
  3.3 1.4 %copy-done.1 = bf16[1024,768]{1,0:T(8,128)(2,1)S(1)} copy-done((bf16[1024,768]{1,0:T(8,128)(2,1)S(1)}, bf16[1024,768]{1,0:T(8,128)(2,1)}, u32[]{:S(2)}) %copy-start.1) | copy-done | bytes 1572888
  4.7 0.0 copy-start.2
  4.7 0.7 copy-done.2
  5.4 85.7 %shard_map.68.total = f32[2,1024,768]{2,1,0:T(8,128)S(1)} custom-call(bf16[1024,768]{1,0:T(8,128)(2,1)S(1)} %copy-done, bf16[1024,768]{1,0:T(8,128)(2,1)S(1)} %copy-done.1, s32[1,1024]{1,0:T(1,128)S(1)} %copy-done.2, f32[1]{0:T(128)S(6)} %copy.7.exponent_ref, f32[1]{0:T(128)S(6)} %copy.8.offset_ref), custom_call_target="tpu_custom_call" | custom-call | flops 17716740096 | bytes 9437184 | tf_op jit(solution)/shard_map/pallas_call | solution.py:206
  91.2 2.7 %shard_map.69 = (f32[1024,768]{1,0:T(8,128)}, f32[1024,768]{1,0:T(8,128)}) custom-call(f32[2,1024,768]{2,1,0:T(8,128)S(1)} %shard_map.68.total), custom_call_target="tpu_custom_call" | custom-call | bytes 12582912 | tf_op jit(solution)/shard_map/pallas_call | solution.py:233
Async XLA Ops:
  1.9 1.4 %copy-start = (bf16[1024,768]{1,0:T(8,128)(2,1)S(1)}, bf16[1024,768]{1,0:T(8,128)(2,1)}, u32[]{:S(2)}) copy-start(bf16[1024,768]{1,0:T(8,128)(2,1)} %text_ref.1) | copy-start | bytes 4718596
  3.3 1.4 %copy-start.1 = (bf16[1024,768]{1,0:T(8,128)(2,1)S(1)}, bf16[1024,768]{1,0:T(8,128)(2,1)}, u32[]{:S(2)}) copy-start(bf16[1024,768]{1,0:T(8,128)(2,1)} %image_ref.1) | copy-start | bytes 4718596
  4.7 0.7 copy-start.2

commit v6 on v5

--- a/solution.py
+++ b/solution.py
@@ -124,8 +124,6 @@
     def place_of(v):
         return lax.rem(v // parts, 2), (v // (2 * parts)) * parts + lax.rem(v, parts)
 
-    own_block(0)
-
     def spread_far(w):
         kind, j = lax.rem(w, 2), w // 2
         for part in range(parts):
@@ -155,9 +153,9 @@
             def _():
                 own_copy(*place_of(v + AHEAD)).start()
 
-            @pl.when((lax.rem(v, parts) == 0) & (u + 1 < rows // UNIT))
+            @pl.when((lax.rem(v, parts) == 1) & (u < rows // UNIT))
             def _():
-                own_block(u + 1)
+                own_block(u)
 
             @pl.when(lax.rem(v, parts) == parts - 1)
             def _():
@@ -228,7 +226,13 @@
         cost_estimate=pl.CostEstimate(
             flops=22 * rows * rows * width, bytes_accessed=12 * rows * width, transcendentals=10 * rows * rows
         ),
-    )(sentence, photo, companion, exponent, offset)
+    )(
+        pltpu.with_memory_space_constraint(sentence, pltpu.HBM),
+        pltpu.with_memory_space_constraint(photo, pltpu.HBM),
+        pltpu.with_memory_space_constraint(companion, pltpu.HBM),
+        exponent,
+        offset,
+    )
     grad = jax.ShapeDtypeStruct((rows, width), jnp.float32)
     text_grad, image_grad = pl.pallas_call(
         move_kernel,

time: 94.1 us -> 87.8 us (0.933)
  local copies, waits for them, and re-layouts: 3.49 us -> 0 us
  Pallas kernels: 88.5 us -> 85.7 us
    unnamed x6 -> x0, local copies, waits for them, and re-layouts: 3.49 us -> none
    pallas_call x1, Pallas kernels: 85.7 us -> 83 us  [local(): pl.pallas_call(functools.partial(kernel, (ring, inner, rows)), out_shape=...]
where the time goes in v6:
time: 87.8 us; the launch traced here: 87.7 us
  Pallas kernels  85.7 us (98%)
  between operations  1.93 us (2%)
    pallas_call x1, Pallas kernels, local(): pl.pallas_call(functools.partial(kernel, (ring, inner, rows)), out_shape=...  83 us
    pallas_call x1, Pallas kernels, local(): pl.pallas_call(move_kernel, out_shape=(grad, grad), in_specs=[vmem], out_...  2.74 us

profile of v6, /device:TPU:0, one launch (start us, length us, event | category | flops | bytes accessed | tf_op | source)
XLA Modules:
  0.0 87.7 jit_solution(16196044596099296460)
XLA Ops:
  1.9 83.0 %shard_map.68.total = f32[2,1024,768]{2,1,0:T(8,128)S(1)} custom-call(bf16[1024,768]{1,0:T(8,128)(2,1)} %text_ref.1, bf16[1024,768]{1,0:T(8,128)(2,1)} %image_ref.1, s32[1,1024]{1,0:T(1,128)} %pair_ref.1, f32[1]{0:T(128)S(6)} %copy.7.exponent_ref, f32[1]{0:T(128)S(6)} %copy.8.offset_ref), custom_call_target="tpu_custom_call" | custom-call | flops 17716740096 | bytes 9437184 | tf_op jit(solution)/shard_map/pallas_call | solution.py:204
  84.9 2.7 %shard_map.69 = (f32[1024,768]{1,0:T(8,128)}, f32[1024,768]{1,0:T(8,128)}) custom-call(f32[2,1024,768]{2,1,0:T(8,128)S(1)} %shard_map.68.total), custom_call_target="tpu_custom_call" | custom-call | bytes 12582912 | tf_op jit(solution)/shard_map/pallas_call | solution.py:237
